TPU v7x, 32 devices: a whole 2x2x4 slice. The times are simulated.
32 devices in a mesh: blk: 8 (over z, x), win: 4 (over y, core).
Axes of the slice: x: 2, y: 2, z: 4, core: 2. Of those that a mesh axis runs over, the one named last changes fastest.
Arguments:
- samples: bfloat16 [1024, 32, 2048], P('blk', 'win'), may hold values from -6 to 6
- pair_offsets: int32 [24], P('blk'), may hold values from 0 to 4, as said below
- pair_count: int32 [8], P('blk'), may hold values from 1 to 3
Outputs:
- cross_spectra: bfloat16 [24, 128, 2, 128, 128], P('blk', 'win')
Inputs may be any that keep to these rules, and one draw needn't show every extreme that they name: `pair_offsets`: entry w * 3 + s belongs to worker w. The live slots of a worker (s below its count) hold different offsets, with w + offset below the number of blocks; the other slots hold 0.
All inputs are finite; a program needn't handle non-finite values.
Results may differ from a plain program's by a relative error of at most 0.0068.
Values may be sent and summed in bfloat16 or wider, within the bound.
A program may use at most 64 MiB of HBM per device.

v0:
```python
import math

import jax
import jax.numpy as jnp
from jax import lax
from jax.sharding import PartitionSpec as P

BINS = 128
BIN0 = 32
SMOOTH = 4
OFFSET = 4


water_level = 0.1
epsilon = 1e-06


def shifted(block, axis, distance):
    devices = range(lax.axis_size(axis))
    route = [(i - distance, i) for i in devices if i - distance in devices]
    return lax.ppermute(block, axis, route)


def dft_table(length):
    sample_idx = jnp.arange(length, dtype=jnp.int32)
    bin_freqs = BIN0 + jnp.arange(BINS, dtype=jnp.int32)
    phases = sample_idx[:, None] * bin_freqs[None, :] % length
    angles = phases.astype(jnp.float32) * (2.0 * math.pi / length)
    window_taper = 0.5 - 0.5 * jnp.cos(
        (sample_idx.astype(jnp.float32) + 0.5) * (2.0 * math.pi / length)
    )
    cosines = window_taper[:, None] * jnp.cos(angles)
    sines = -window_taper[:, None] * jnp.sin(angles)
    return jnp.concatenate([cosines, sines], axis=1).astype(jnp.bfloat16)


def band_weights():
    bin_index = jnp.arange(BINS, dtype=jnp.int32)
    inside = (jnp.abs(bin_index[:, None] - bin_index[None, :]) <= SMOOTH).astype(jnp.float32)
    return inside / jnp.sum(inside, axis=0, keepdims=True)


def whiten_spectrum(spectrum, weights):
    energy = spectrum[:, 0] * spectrum[:, 0] + spectrum[:, 1] * spectrum[:, 1]
    smoothed = jnp.einsum("wjc,jb->wbc", energy, weights, precision=lax.Precision.HIGHEST)
    average = jnp.mean(energy, axis=1, keepdims=True)
    factor = lax.rsqrt(smoothed + water_level * average + epsilon)
    return (spectrum * factor[:, None]).astype(jnp.bfloat16)


def cross_pair(left_side, partner, windows):
    right_side = partner.reshape(2 * windows, partner.shape[2], partner.shape[3])
    product = lax.dot_general(
        left_side, right_side, (((1,), (0,)), ((2,), (1,))), preferred_element_type=jnp.float32
    )
    return product * (1.0 / windows)


def shards(samples, pair_offsets, pair_count):
    channels, win_dev, length = samples.shape
    table = dft_table(length)
    weights = band_weights()
    spectrum = jnp.einsum("cwt,tk->wkc", samples, table, preferred_element_type=jnp.float32)
    whitened = whiten_spectrum(spectrum.reshape(win_dev, 2, BINS, channels), weights)
    by_bins = lax.all_to_all(whitened, "win", split_axis=2, concat_axis=0, tiled=True)
    windows = by_bins.shape[0]
    bins_dev = by_bins.shape[2]
    swapped = jnp.stack([by_bins[:, 1], -by_bins[:, 0]], axis=1)
    left_side = jnp.stack([by_bins, swapped], axis=0).reshape(2, 2 * windows, bins_dev, channels)
    neighbours = [by_bins]
    for distance in range(1, OFFSET + 1):
        neighbours.append(shifted(by_bins, "blk", -distance))
    nearby = jnp.stack(neighbours, axis=0)
    live_count = pair_count[0]
    slot_total = pair_offsets.shape[0]
    results = []
    for slot_rank in range(slot_total):
        partner = lax.dynamic_index_in_dim(nearby, pair_offsets[slot_rank], 0, keepdims=False)
        value = cross_pair(left_side, partner, windows)
        results.append(
            jnp.where(slot_rank < live_count, value, jnp.zeros_like(value)).astype(jnp.bfloat16)
        )
    cross_spectra = jnp.stack(results, axis=0)
    return cross_spectra


def solution(mesh):
    in_specs = (P("blk", "win", None), P("blk"), P("blk"))
    out_specs = P("blk", "win", None, None, None)
    return jax.shard_map(shards, mesh=mesh, in_specs=in_specs, out_specs=out_specs, check_vma=False)
```

profile of v0, /device:TPU:0, one launch (start us, length us, event | category | flops | bytes accessed | tf_op | source)
XLA Modules:
  0.0 109.8 jit_solution(9315533526000073080)
XLA Ops:
  0.0 0.1 convert_reduce_fusion
  0.1 0.1 multiply_subtract_fusion
  0.2 4.5 %multiply_convert_fusion.2 = (bf16[2048,128]{0,1:T(8,128)(2,1)S(1)}, bf16[2048,128]{0,1:T(8,128)(2,1)S(1)}) fusion(s32[128]{0:T(128)S(1)} %iota_add_fusion, f32[2048]{0:T(1024)S(1)} %get-tuple-element.15, f32[2048]{0:T(1024)S(1)} %get-tuple-element.16), kind=kLoop, calls=%fused_computation.25 | loop fusion | flops 4718592 | bytes 1065472 | tf_op jit(solution)/shard_map/convert
  4.7 7.1 %fusion = f32[256,128,8]{1,0,2:T(8,128)S(1)} fusion(bf16[128,8,2048]{2,1,0:T(8,128)(2,1)} %param.3, bf16[2048,128]{0,1:T(8,128)(2,1)S(1)} %get-tuple-element.14, bf16[2048,128]{0,1:T(8,128)(2,1)S(1)} %get-tuple-element.13), kind=kOutput, calls=%fused_computation.1 | convolution fusion | flops 1075838976 | bytes 6291456 | tf_op jit(solution)/shard_map/cwt,tk->wkc/dot_general | solution.py:63
  11.9 0.1 fusion.18
  12.0 0.0 copy-start
  12.0 0.6 fusion.7
  12.7 0.1 multiply_convert_fusion
  12.8 1.3 %copy.15 = bf16[8,2,128,128]{3,1,0,2:T(2,128)(2,1)} copy(bf16[8,2,128,128]{3,2,1,0:T(8,128)(2,1)S(1)} %multiply_convert_fusion) | data formatting | bytes 1048576 | tf_op jit(solution)/shard_map/convert_element_type | solution.py:48
  14.1 4.2 %all-to-all-start = ((bf16[8,2,128,128]{3,1,0,2:T(2,128)(2,1)}), bf16[8,2,128,128]{3,1,0,2:T(2,128)(2,1)S(1)}, u32[]{:S(2)}, u32[]{:S(2)}) async-start(bf16[8,2,128,128]{3,1,0,2:T(2,128)(2,1)} %copy.15), calls=%async_computation | async-start | bytes 1048576 | tf_op jit(solution)/shard_map/all_to_all | solution.py:65
  18.3 0.0 copy-done
  18.3 0.7 fusion.31
  25.2 1.9 %all-to-all-done = bf16[8,2,128,128]{3,1,0,2:T(2,128)(2,1)S(1)} async-done(((bf16[8,2,128,128]{3,1,0,2:T(2,128)(2,1)}), bf16[8,2,128,128]{3,1,0,2:T(2,128)(2,1)S(1)}, u32[]{:S(2)}, u32[]{:S(2)}) %all-to-all-start) | async-done | bytes 524320 | tf_op jit(solution)/shard_map/all_to_all | solution.py:65
  27.2 0.5 copy.16
  27.7 1.3 %collective-permute-start.2 = (bf16[32,2,32,128]{3,1,0,2:T(2,128)(2,1)S(1)}, bf16[32,2,32,128]{3,1,0,2:T(2,128)(2,1)S(1)}, u32[]{:S(2)}, u32[]{:S(2)}) collective-permute-start(bf16[32,2,32,128]{3,1,0,2:T(2,128)(2,1)S(1)} %bitcast.62), channel_id=1, source_target_pairs={{12,0},{16,4},{20,8},{24,12},{28,16},{13,1},{17,5},{21,9},{25,13},... | collective-permute-start | bytes 1572872 | tf_op jit(solution)/shard_map/ppermute | solution.py:21
  29.0 1.3 %collective-permute-start.1 = (bf16[32,2,32,128]{3,1,0,2:T(2,128)(2,1)S(1)}, bf16[32,2,32,128]{3,1,0,2:T(2,128)(2,1)S(1)}, u32[]{:S(2)}, u32[]{:S(2)}) collective-permute-start(bf16[32,2,32,128]{3,1,0,2:T(2,128)(2,1)S(1)} %bitcast.63), channel_id=1, source_target_pairs={{8,0},{12,4},{16,8},{20,12},{24,16},{28,20},{9,1},{13,5},{17,9},{2... | collective-permute-start | bytes 1572872 | tf_op jit(solution)/shard_map/ppermute | solution.py:21
  30.3 1.3 %collective-permute-start = (bf16[32,2,32,128]{3,1,0,2:T(2,128)(2,1)S(1)}, bf16[32,2,32,128]{3,1,0,2:T(2,128)(2,1)S(1)}, u32[]{:S(2)}, u32[]{:S(2)}) collective-permute-start(bf16[32,2,32,128]{3,1,0,2:T(2,128)(2,1)S(1)} %bitcast.64), channel_id=1, source_target_pairs={{4,0},{8,4},{12,8},{16,12},{20,16},{24,20},{28,24},{5,1},{9,5},{13... | collective-permute-start | bytes 1572872 | tf_op jit(solution)/shard_map/ppermute | solution.py:21
  31.6 1.5 %collective-permute-start.3 = (bf16[32,2,32,128]{3,1,0,2:T(2,128)(2,1)S(1)}, bf16[32,2,32,128]{3,1,0,2:T(2,128)(2,1)S(1)}, u32[]{:S(2)}, u32[]{:S(2)}) collective-permute-start(bf16[32,2,32,128]{3,1,0,2:T(2,128)(2,1)S(1)} %bitcast.65), channel_id=1, source_target_pairs={{16,0},{20,4},{24,8},{28,12},{17,1},{21,5},{25,9},{29,13},{18,2},{... | collective-permute-start | bytes 1572872 | tf_op jit(solution)/shard_map/ppermute | solution.py:21
  33.1 0.9 fusion.30
  34.1 0.4 constant_dynamic-update-slice_fusion
  34.5 1.2 %pad_maximum_fusion.2 = bf16[32,2,32,128]{3,1,0,2:T(2,128)(2,1)S(1)} fusion(bf16[32,1,32,128]{3,1,0,2:T(2,128)(2,1)S(1)} %get-tuple-element.9, bf16[32,1,32,128]{3,1,0,2:T(2,128)(2,1)S(1)} %get-tuple-element.8), kind=kLoop, calls=%fused_computation.33 | loop fusion | flops 1048576 | bytes 1048576 | tf_op jit(solution)/shard_map/stack | solution.py:68
  35.7 20.0 %collective-permute-done = bf16[32,2,32,128]{3,1,0,2:T(2,128)(2,1)S(1)} collective-permute-done((bf16[32,2,32,128]{3,1,0,2:T(2,128)(2,1)S(1)}, bf16[32,2,32,128]{3,1,0,2:T(2,128)(2,1)S(1)}, u32[]{:S(2)}, u32[]{:S(2)}) %collective-permute-start) | collective-permute-done | bytes 524320 | tf_op jit(solution)/shard_map/ppermute | solution.py:21
  55.7 0.5 bitcast_dynamic-update-slice_fusion.3
  56.2 0.0 collective-permute-done.1
  56.3 0.5 bitcast_dynamic-update-slice_fusion.2
  56.8 0.0 collective-permute-done.2
  56.8 0.5 bitcast_dynamic-update-slice_fusion.1
  57.3 44.6 %collective-permute-done.3 = bf16[32,2,32,128]{3,1,0,2:T(2,128)(2,1)S(1)} collective-permute-done((bf16[32,2,32,128]{3,1,0,2:T(2,128)(2,1)S(1)}, bf16[32,2,32,128]{3,1,0,2:T(2,128)(2,1)S(1)}, u32[]{:S(2)}, u32[]{:S(2)}) %collective-permute-start.3) | collective-permute-done | bytes 524320 | tf_op jit(solution)/shard_map/ppermute | solution.py:21
  101.8 0.5 bitcast_dynamic-update-slice_fusion
  102.3 1.5 %constant_dynamic-slice_fusion.2 = (bf16[1,32,2,32,128]{4,2,1,3,0:T(2,128)(2,1)S(1)}, bf16[1,32,2,32,128]{4,2,1,3,0:T(2,128)(2,1)S(1)}, bf16[1,32,2,32,128]{4,2,1,3,0:T(2,128)(2,1)S(1)}) fusion(bf16[5,32,2,32,128]{4,2,1,3,0:T(2,128)(2,1)S(1)} %bitcast_dynamic-update-slice_fusion, s32[]{:T(128)S(6)} %select_n.41, s32[]{:T(128)S(6)} %select_n.47, s32[]{:T(128)S(6)} %select_n.44), kind=kLoop, calls=%fused_computation.52 | loop fusion | bytes 3145740 | tf_op jit(solution)/shard_map/jit(dynamic_index_in_dim)/dynamic_slice | solution.py:78
  103.8 0.9 fusion.4
  104.7 0.9 fusion.2
  105.7 0.9 fusion.3
  106.6 3.2 %pad_maximum_fusion = bf16[3,32,2,128,128]{4,3,2,1,0:T(8,128)(2,1)} fusion(bf16[1,32,2,128,128]{4,3,2,1,0:T(8,128)(2,1)S(1)} %fusion.4, bf16[1,32,2,128,128]{4,3,2,1,0:T(8,128)(2,1)S(1)} %fusion.3, bf16[1,32,2,128,128]{4,3,2,1,0:T(8,128)(2,1)S(1)} %fusion.2), kind=kLoop, calls=%fused_computation | loop fusion | flops 6291456 | bytes 12582912 | tf_op jit(solution)/shard_map/stack | solution.py:83
  (2 shorter events, 0.0 us)
Async XLA Ops:
  12.0 6.4 %copy-start = (s32[3]{0:T(128)S(1)}, s32[3]{0:T(128)}, u32[]{:S(2)}) copy-start(s32[3]{0:T(128)} %param.4) | copy-start | bytes 40
  14.1 13.1 %all-to-all-start = ((bf16[8,2,128,128]{3,1,0,2:T(2,128)(2,1)}), bf16[8,2,128,128]{3,1,0,2:T(2,128)(2,1)S(1)}, u32[]{:S(2)}, u32[]{:S(2)}) async-start(bf16[8,2,128,128]{3,1,0,2:T(2,128)(2,1)} %copy.15), calls=%async_computation | async-start | bytes 1048576 | tf_op jit(solution)/shard_map/all_to_all | solution.py:65
  27.7 29.0 %collective-permute-start.2 = (bf16[32,2,32,128]{3,1,0,2:T(2,128)(2,1)S(1)}, bf16[32,2,32,128]{3,1,0,2:T(2,128)(2,1)S(1)}, u32[]{:S(2)}, u32[]{:S(2)}) collective-permute-start(bf16[32,2,32,128]{3,1,0,2:T(2,128)(2,1)S(1)} %bitcast.62), channel_id=1, source_target_pairs={{12,0},{16,4},{20,8},{24,12},{28,16},{13,1},{17,5},{21,9},{25,13},... | collective-permute-start | bytes 1572872 | tf_op jit(solution)/shard_map/ppermute | solution.py:21
  29.0 27.2 %collective-permute-start.1 = (bf16[32,2,32,128]{3,1,0,2:T(2,128)(2,1)S(1)}, bf16[32,2,32,128]{3,1,0,2:T(2,128)(2,1)S(1)}, u32[]{:S(2)}, u32[]{:S(2)}) collective-permute-start(bf16[32,2,32,128]{3,1,0,2:T(2,128)(2,1)S(1)} %bitcast.63), channel_id=1, source_target_pairs={{8,0},{12,4},{16,8},{20,12},{24,16},{28,20},{9,1},{13,5},{17,9},{2... | collective-permute-start | bytes 1572872 | tf_op jit(solution)/shard_map/ppermute | solution.py:21
  30.3 25.4 %collective-permute-start = (bf16[32,2,32,128]{3,1,0,2:T(2,128)(2,1)S(1)}, bf16[32,2,32,128]{3,1,0,2:T(2,128)(2,1)S(1)}, u32[]{:S(2)}, u32[]{:S(2)}) collective-permute-start(bf16[32,2,32,128]{3,1,0,2:T(2,128)(2,1)S(1)} %bitcast.64), channel_id=1, source_target_pairs={{4,0},{8,4},{12,8},{16,12},{20,16},{24,20},{28,24},{5,1},{9,5},{13... | collective-permute-start | bytes 1572872 | tf_op jit(solution)/shard_map/ppermute | solution.py:21
  31.6 70.2 %collective-permute-start.3 = (bf16[32,2,32,128]{3,1,0,2:T(2,128)(2,1)S(1)}, bf16[32,2,32,128]{3,1,0,2:T(2,128)(2,1)S(1)}, u32[]{:S(2)}, u32[]{:S(2)}) collective-permute-start(bf16[32,2,32,128]{3,1,0,2:T(2,128)(2,1)S(1)} %bitcast.65), channel_id=1, source_target_pairs={{16,0},{20,4},{24,8},{28,12},{17,1},{21,5},{25,9},{29,13},{18,2},{... | collective-permute-start | bytes 1572872 | tf_op jit(solution)/shard_map/ppermute | solution.py:21
where the time goes:
time: 110 us
  waiting for transfers between devices  66.6 us (61%)
  matrix products  10.6 us (10%)
  other arithmetic  10.2 us (9%)
  starting transfers between devices  9.58 us (9%)
  between operations  6.46 us (6%)
  local copies, waits for them, and re-layouts  6.39 us (6%)
    ppermute x4, waiting for transfers between devices, shifted(): return lax.ppermute(block, axis, route)  64.6 us
    dot_general x1, matrix products, shards(): jnp.einsum('cwt,tk->wkc', samples, table, preferred_element_type=jnp.floa...  7.15 us
    ppermute x4, starting transfers between devices, shifted(): return lax.ppermute(block, axis, route)  5.35 us
    another operation x1, other arithmetic  4.53 us
    all_to_all x1, starting transfers between devices, shards(): lax.all_to_all(whitened, 'win', split_axis=2, concat_axis=0, tiled=True)  4.24 us
    another operation x1, other arithmetic, shards(): cross_spectra = jnp.stack(results, axis=0)  3.15 us
    dot_general x3, matrix products, cross_pair(): lax.dot_general(left_side, right_side, (((1,), (0,)), ((2,), (1,))), pref...  2.8 us
  transfers between devices with their start and end apart: 5, of which 3 were waited for; matrix products, arithmetic and copies ran while one was open for 4% of the time, Pallas kernels for 0%

commit v1 on v0

v1 whole, which is shorter than its diff:
```python
import functools
import math

import jax
import jax.numpy as jnp
import ml_dtypes
import numpy as np
from jax import lax
from jax.experimental import pallas as pl
from jax.experimental.pallas import tpu as pltpu
from jax.sharding import PartitionSpec as P

BINS = 128
BIN0 = 32
SMOOTH = 4
OFFSET = 4

WATER_LEVEL = 0.1
EPSILON = 1e-06

ROW_STEPS = 4
CHUNKS = 4
BIN_BLOCK = 4
VMEM_LIMIT = 40 * 1024 * 1024
MESH = pl.DeviceIdType.MESH


def dft_table(length):
    sample_idx = np.arange(length, dtype=np.int64)
    bin_freqs = BIN0 + np.arange(BINS, dtype=np.int64)
    angles = (sample_idx[:, None] * bin_freqs[None, :] % length) * (2.0 * math.pi / length)
    taper = 0.5 - 0.5 * np.cos((sample_idx + 0.5) * (2.0 * math.pi / length))
    table = np.concatenate(
        [taper[:, None] * np.cos(angles), -taper[:, None] * np.sin(angles)], axis=1
    )
    return table.astype(np.float32).astype(ml_dtypes.bfloat16)


def band_table():
    idx = np.arange(BINS)
    inside = (np.abs(idx[:, None] - idx[None, :]) <= SMOOTH).astype(np.float32)
    band = np.concatenate([inside, np.ones((BINS, BINS), np.float32)], axis=1)
    scale = np.concatenate(
        [1.0 / inside.sum(axis=0), np.full((BINS,), WATER_LEVEL / BINS, np.float32)]
    )
    return band.astype(ml_dtypes.bfloat16), scale.astype(np.float32)[None, :]


def whiten_kernel(wins, samples_ref, table_ref, band_ref, scale_ref, out_ref, white, turned):
    step = pl.program_id(0)
    rows = samples_ref.shape[0]
    channels = white.shape[1] // wins
    spectrum = jnp.dot(samples_ref[...], table_ref[...], preferred_element_type=jnp.float32)
    real, imag = spectrum[:, :BINS], spectrum[:, BINS:]
    energy = real * real + imag * imag
    sums = jnp.dot(
        energy.astype(jnp.bfloat16), band_ref[...], preferred_element_type=jnp.float32
    ) * scale_ref[...]
    factor = lax.rsqrt(sums[:, :BINS] + sums[:, BINS:] + EPSILON)
    here = pl.ds(pl.multiple_of(step * rows, rows), rows)
    white[0, here, :] = real * factor
    white[1, here, :] = imag * factor

    @pl.when(step == pl.num_programs(0) - 1)
    def _():
        for part in range(2):
            for win in range(wins):
                piece = white[part, pl.ds(win, channels, stride=wins), :]
                turned[pl.ds(part * wins + win, BINS, stride=2 * wins), :] = piece.T
        out_ref[...] = turned[...].reshape(out_ref.shape).astype(jnp.bfloat16)


def whiten(samples):
    channels, wins, length = samples.shape
    rows = channels * wins
    table = jnp.asarray(dft_table(length))
    band, scale = band_table()
    step_rows = rows // ROW_STEPS
    return pl.pallas_call(
        functools.partial(whiten_kernel, wins),
        grid=(ROW_STEPS,),
        in_specs=[
            pl.BlockSpec((step_rows, length), lambda i: (i, 0)),
            pl.BlockSpec((length, 2 * BINS), lambda i: (0, 0)),
            pl.BlockSpec((BINS, 2 * BINS), lambda i: (0, 0)),
            pl.BlockSpec((1, 2 * BINS), lambda i: (0, 0)),
        ],
        out_specs=pl.BlockSpec((BINS, 2 * wins, channels), lambda i: (0, 0, 0)),
        out_shape=jax.ShapeDtypeStruct((BINS, 2 * wins, channels), jnp.bfloat16),
        scratch_shapes=[
            pltpu.VMEM((2, rows, BINS), jnp.float32),
            pltpu.VMEM((BINS * 2 * wins, channels), jnp.float32),
        ],
        compiler_params=pltpu.CompilerParams(vmem_limit_bytes=VMEM_LIMIT),
        name="whiten",
    )(samples.reshape(rows, length), table, jnp.asarray(band), jnp.asarray(scale))


def exchange_kernel(
    nb, nw, send_ref, near_ref, home_sem, a_send, a_recv, z_send, z_recv, x_send, x_recv
):
    worker, group = lax.axis_index("blk"), lax.axis_index("win")
    level, odd = lax.div(worker, 2), lax.rem(worker, 2)
    levels = nb // 2
    partner = worker + 1 - 2 * odd
    has_below = level >= 1
    has_one = level + 1 < levels
    has_two = level + 2 < levels
    is_even, is_odd = odd == 0, odd == 1
    bins_dev = near_ref.shape[1]
    rows = send_ref.shape[1]
    size = bins_dev // CHUNKS

    barrier = pltpu.get_barrier_semaphore()

    def greet(device):
        pl.semaphore_signal(barrier, inc=1, device_id=device, device_id_type=MESH)

    peers = [lax.rem(group + k, nw) for k in range(1, nw)]
    for peer in peers:
        greet({"win": peer})
    greet({"blk": partner})

    @pl.when(has_below)
    def _():
        greet({"blk": worker - 2})

    @pl.when(has_one)
    def _():
        greet({"blk": worker + 2})

    my_rows = pl.ds(pl.multiple_of(group * rows, rows), rows)
    home = pltpu.make_async_copy(
        send_ref.at[pl.ds(group * bins_dev, bins_dev)], near_ref.at[0, :, my_rows], home_sem
    )
    home.start()
    pl.semaphore_wait(barrier, nw + has_below.astype(jnp.int32) + has_one.astype(jnp.int32))

    def spread(k, c):
        return pltpu.make_async_remote_copy(
            src_ref=send_ref.at[pl.ds(peers[k] * bins_dev + c * size, size)],
            dst_ref=near_ref.at[0, pl.ds(c * size, size), my_rows],
            send_sem=a_send.at[k, c],
            recv_sem=a_recv.at[k, c],
            device_id={"win": peers[k]},
            device_id_type=MESH,
        )

    def move(src, dst, device, send, recv, at, c):
        return pltpu.make_async_remote_copy(
            src_ref=near_ref.at[src, pl.ds(c * size, size)],
            dst_ref=near_ref.at[dst, pl.ds(c * size, size)],
            send_sem=send.at[at, c],
            recv_sem=recv.at[at, c],
            device_id={"blk": device},
            device_id_type=MESH,
        )

    def down(at, c):
        return move(2 * at, 2 * at + 2, worker - 2, z_send, z_recv, at, c)

    def across(at, c):
        return move(2 * at + 2 * (1 - odd), 2 * at + 1, partner, x_send, x_recv, at, c)

    for c in range(CHUNKS):
        for k in range(nw - 1):
            spread(k, c).start()
    home.wait()

    def own_part(c):
        for k in range(nw - 1):
            spread(k, c).wait_recv()

        @pl.when(has_below)
        def _():
            down(0, c).start()

        @pl.when(is_odd)
        def _():
            across(0, c).start()

    def second_part(c):
        @pl.when(has_one)
        def _():
            down(0, c).wait_recv()

            @pl.when(has_below)
            def _():
                down(1, c).start()

            @pl.when(is_even)
            def _():
                across(0, c).start()

            @pl.when(is_odd)
            def _():
                across(1, c).start()

    def fourth_part(c):
        @pl.when(has_two)
        def _():
            down(1, c).wait_recv()

            @pl.when(is_even)
            def _():
                across(1, c).start()

    own_part(0)
    for c in range(1, CHUNKS):
        own_part(c)
        second_part(c - 1)
    second_part(CHUNKS - 1)
    for c in range(CHUNKS):
        fourth_part(c)

    first_live = jnp.logical_or(is_even, has_one)
    third_live = jnp.logical_or(jnp.logical_and(is_even, has_one), has_two)
    first_sent = jnp.logical_or(is_odd, has_one)
    third_sent = jnp.logical_or(jnp.logical_and(is_odd, has_one), has_two)
    both = jnp.logical_and(has_below, has_one)
    for c in range(CHUNKS):
        for k in range(nw - 1):
            spread(k, c).wait_send()

        @pl.when(first_live)
        def _():
            across(0, c).wait_recv()

        @pl.when(third_live)
        def _():
            across(1, c).wait_recv()

        @pl.when(has_below)
        def _():
            down(0, c).wait_send()

        @pl.when(both)
        def _():
            down(1, c).wait_send()

        @pl.when(first_sent)
        def _():
            across(0, c).wait_send()

        @pl.when(third_sent)
        def _():
            across(1, c).wait_send()


def exchange(white, nb, nw):
    bins, rows, channels = white.shape
    return pl.pallas_call(
        functools.partial(exchange_kernel, nb, nw),
        in_specs=[pl.BlockSpec(memory_space=pl.ANY)],
        out_specs=pl.BlockSpec(memory_space=pl.ANY),
        out_shape=jax.ShapeDtypeStruct(
            (OFFSET + 1, bins // nw, nw * rows, channels), jnp.bfloat16
        ),
        scratch_shapes=[
            pltpu.SemaphoreType.DMA,
            pltpu.SemaphoreType.DMA((nw - 1, CHUNKS)),
            pltpu.SemaphoreType.DMA((nw - 1, CHUNKS)),
            pltpu.SemaphoreType.DMA((2, CHUNKS)),
            pltpu.SemaphoreType.DMA((2, CHUNKS)),
            pltpu.SemaphoreType.DMA((2, CHUNKS)),
            pltpu.SemaphoreType.DMA((2, CHUNKS)),
        ],
        compiler_params=pltpu.CompilerParams(collective_id=0, has_side_effects=True),
        name="exchange",
    )(white)


def cross_kernel(half, windows, offsets_ref, count_ref, own_ref, *refs):
    partners, out_ref = refs[:-1], refs[-1]
    scales = [
        jnp.where(s < count_ref[0], 1.0 / windows, 0.0).astype(jnp.float32)
        for s in range(len(partners))
    ]
    depth, channels = own_ref.shape[2], own_ref.shape[3]
    for b in range(own_ref.shape[1]):
        mine = own_ref[0, b].astype(jnp.float32)
        split = mine.reshape(depth // (2 * half), 2, half, channels)
        swapped = jnp.stack([split[:, 1], -split[:, 0]], axis=1).reshape(depth, channels)
        left = jnp.concatenate([mine.T, swapped.T], axis=0).astype(jnp.bfloat16)
        for s, partner in enumerate(partners):
            value = jnp.dot(left, partner[0, b], preferred_element_type=jnp.float32) * scales[s]
            out_ref[s, b] = value.reshape(2, channels, channels).astype(jnp.bfloat16)


def cross(near, pair_offsets, pair_count, wins):
    _, bins_dev, depth, channels = near.shape
    slots = pair_offsets.shape[0]

    def partner_spec(s):
        return pl.BlockSpec(
            (1, BIN_BLOCK, depth, channels), lambda i, offsets, count: (offsets[s], i, 0, 0)
        )

    return pl.pallas_call(
        functools.partial(cross_kernel, wins, depth // 2),
        grid_spec=pltpu.PrefetchScalarGridSpec(
            num_scalar_prefetch=2,
            grid=(bins_dev // BIN_BLOCK,),
            in_specs=[
                pl.BlockSpec((1, BIN_BLOCK, depth, channels), lambda i, offsets, count: (0, i, 0, 0))
            ]
            + [partner_spec(s) for s in range(slots)],
            out_specs=pl.BlockSpec(
                (slots, BIN_BLOCK, 2, channels, channels),
                lambda i, offsets, count: (0, i, 0, 0, 0),
            ),
        ),
        out_shape=jax.ShapeDtypeStruct((slots, bins_dev, 2, channels, channels), jnp.bfloat16),
        compiler_params=pltpu.CompilerParams(vmem_limit_bytes=VMEM_LIMIT),
        name="cross",
    )(pair_offsets, pair_count, *([near] * (slots + 1)))


def shards(nb, nw, samples, pair_offsets, pair_count):
    white = whiten(samples)
    near = exchange(white, nb, nw)
    return cross(near, pair_offsets, pair_count, samples.shape[1])


def solution(mesh):
    body = functools.partial(shards, mesh.shape["blk"], mesh.shape["win"])
    in_specs = (P("blk", "win", None), P("blk"), P("blk"))
    out_specs = P("blk", "win", None, None, None)
    return jax.shard_map(body, mesh=mesh, in_specs=in_specs, out_specs=out_specs, check_vma=False)
```

time: 110 us -> 59.8 us (0.54)
  waiting for transfers between devices: 66.6 us -> 0 us
  Pallas kernels: 0 us -> 51.3 us
  matrix products: 10.6 us -> 0 us
  other arithmetic: 10.2 us -> 0 us
  starting transfers between devices: 9.58 us -> 0 us
  between operations: 6.46 us -> 0.71 us
    ppermute x4 -> x0, waiting for transfers between devices: 64.6 us -> none  [shifted(): return lax.ppermute(block, axis, route)]
    pallas_call x0 -> x3, Pallas kernels: none -> 51.3 us  [the longest x1 42.1 us: exchange(): pl.pallas_call(functools.partial(exchange_kernel, nb, nw), in_specs=[pl.B...]
    dot_general x5 -> x0, matrix products: 10.6 us -> none  [the longest x1 7.15 us: shards(): jnp.einsum('cwt,tk->wkc', samples, table, preferred_element_type=jnp.floa...]
    another operation x3 -> x0, other arithmetic: 8.88 us -> none
    unnamed x6 -> x14, local copies, waits for them, and re-layouts: 1.92 us -> 7.45 us
    ppermute x4 -> x0, starting transfers between devices: 5.35 us -> none  [shifted(): return lax.ppermute(block, axis, route)]
    all_to_all x1 -> x0, starting transfers between devices: 4.24 us -> none  [shards(): lax.all_to_all(whitened, 'win', split_axis=2, concat_axis=0, tiled=True)]
    all_to_all x1 -> x0, waiting for transfers between devices: 1.94 us -> none  [shards(): lax.all_to_all(whitened, 'win', split_axis=2, concat_axis=0, tiled=True)]
  transfers between devices with their start and end apart: 5 -> 0, of which waited for: 3 -> 0; matrix products, arithmetic and copies ran while one was open for 4% -> 0% of each run, Pallas kernels for 0% -> 0%
where the time goes in v1:
time: 59.8 us; the launch traced here: 59.5 us
  Pallas kernels  51.3 us (86%)
  local copies, waits for them, and re-layouts  7.45 us (12%)
  between operations  0.71 us (1%)
    pallas_call x1, Pallas kernels, exchange(): pl.pallas_call(functools.partial(exchange_kernel, nb, nw), in_specs=[pl.B...  42.1 us
    unnamed x14, local copies, waits for them, and re-layouts  7.45 us
    pallas_call x1, Pallas kernels, cross(): pl.pallas_call(functools.partial(cross_kernel, wins, depth // 2), grid_sp...  6.29 us
    pallas_call x1, Pallas kernels, whiten(): pl.pallas_call(functools.partial(whiten_kernel, wins), grid=(ROW_STEPS,),...  2.95 us

profile of v1, /device:TPU:0, one launch (start us, length us, event | category | flops | bytes accessed | tf_op | source)
XLA Modules:
  0.0 59.5 jit_solution(15789012884965626581)
XLA Ops:
  0.7 0.0 copy-start.1
  0.7 2.2 %copy-done.1 = bf16[128,8,2048]{2,1,0:T(8,128)(2,1)S(1)} copy-done((bf16[128,8,2048]{2,1,0:T(8,128)(2,1)S(1)}, bf16[128,8,2048]{2,1,0:T(8,128)(2,1)}, u32[]{:S(2)}) %copy-start.1) | copy-done | bytes 4194328
  2.8 0.0 copy-start.3
  2.8 1.2 %copy-done.3 = bf16[2048,256]{1,0:T(8,128)(2,1)S(1)} copy-done((bf16[2048,256]{1,0:T(8,128)(2,1)S(1)}, bf16[2048,256]{1,0:T(8,128)(2,1)}, u32[]{:S(2)}) %copy-start.3) | copy-done | bytes 1048600
  4.1 0.0 copy-start.4
  4.1 0.8 %copy-done.4 = bf16[128,256]{1,0:T(8,128)(2,1)S(1)} copy-done((bf16[128,256]{1,0:T(8,128)(2,1)S(1)}, bf16[128,256]{1,0:T(8,128)(2,1)}, u32[]{:S(2)}) %copy-start.4) | copy-done | bytes 65560
  4.9 0.0 copy-start.5
  4.9 0.7 %copy-done.5 = f32[1,256]{1,0:T(1,128)S(1)} copy-done((f32[1,256]{1,0:T(1,128)S(1)}, f32[1,256]{1,0:T(1,128)}, u32[]{:S(2)}) %copy-start.5) | copy-done | bytes 1048
  5.6 0.0 copy-start.6
  5.6 3.0 %whiten.1.send_ref = bf16[128,16,128]{2,1,0:T(8,128)(2,1)S(1)} custom-call(bf16[1024,2048]{1,0:T(8,128)(2,1)S(1)} %bitcast.1, bf16[2048,256]{1,0:T(8,128)(2,1)S(1)} %copy-done.3, bf16[128,256]{1,0:T(8,128)(2,1)S(1)} %copy-done.4, f32[1,256]{1,0:T(1,128)S(1)} %copy-done.5), custom_call_target="tpu_custom_call" | custom-call | tf_op jit(solution)/shard_map/whiten/pallas_call | solution.py:79
  8.6 0.0 copy-start.2
  8.6 0.8 %copy-done.2 = bf16[128,16,128]{2,1,0:T(8,128)(2,1)} copy-done((bf16[128,16,128]{2,1,0:T(8,128)(2,1)}, bf16[128,16,128]{2,1,0:T(8,128)(2,1)S(1)}, u32[]{:S(2)}) %copy-start.2) | copy-done | bytes 524312
  9.3 42.1 %exchange.1.own_ref.refs_0_.refs_1_.refs_2_ = bf16[5,32,64,128]{3,2,1,0:T(8,128)(2,1)} custom-call(bf16[128,16,128]{2,1,0:T(8,128)(2,1)} %copy-done.2), custom_call_target="tpu_custom_call" | custom-call | tf_op jit(solution)/shard_map/exchange/pallas_call | solution.py:252
  51.4 0.0 copy-done.6
  51.4 0.0 copy-start
  51.4 1.7 %copy-done = bf16[5,32,64,128]{3,2,1,0:T(8,128)(2,1)S(1)} copy-done((bf16[5,32,64,128]{3,2,1,0:T(8,128)(2,1)S(1)}, bf16[5,32,64,128]{3,2,1,0:T(8,128)(2,1)}, u32[]{:S(2)}) %copy-start) | copy-done | bytes 2621464
  53.2 6.3 %cross.1 = bf16[3,32,2,128,128]{4,3,2,1,0:T(8,128)(2,1)} custom-call(s32[3]{0:T(128)S(1)} %copy-done.6, s32[1]{0:T(128)S(6)} %copy.7.count_ref, bf16[5,32,64,128]{3,2,1,0:T(8,128)(2,1)S(1)} %copy-done, bf16[5,32,64,128]{3,2,1,0:T(8,128)(2,1)S(1)} %copy-done, bf16[5,32,64,128]{3,2,1,0:T(8,128)(2,1)S(1)} %copy-done, bf16[5,32,64,128]{3,2,1,0:T(8,128)(2,1)S(1)} %copy-done), custom_call_target="tpu_custom_call" | custom-call | tf_op jit(solution)/shard_map/cross/pallas_call | solution.py:299
Async XLA Ops:
  0.7 2.2 %copy-start.1 = (bf16[128,8,2048]{2,1,0:T(8,128)(2,1)S(1)}, bf16[128,8,2048]{2,1,0:T(8,128)(2,1)}, u32[]{:S(2)}) copy-start(bf16[128,8,2048]{2,1,0:T(8,128)(2,1)} %param.6) | copy-start | bytes 12582916
  2.8 1.2 %copy-start.3 = (bf16[2048,256]{1,0:T(8,128)(2,1)S(1)}, bf16[2048,256]{1,0:T(8,128)(2,1)}, u32[]{:S(2)}) copy-start(bf16[2048,256]{1,0:T(8,128)(2,1)} %constant.6.clone.table_ref) | copy-start | bytes 3145732
  4.1 0.8 %copy-start.4 = (bf16[128,256]{1,0:T(8,128)(2,1)S(1)}, bf16[128,256]{1,0:T(8,128)(2,1)}, u32[]{:S(2)}) copy-start(bf16[128,256]{1,0:T(8,128)(2,1)} %constant.7.clone.band_ref) | copy-start | bytes 196612
  4.9 0.7 %copy-start.5 = (f32[1,256]{1,0:T(1,128)S(1)}, f32[1,256]{1,0:T(1,128)}, u32[]{:S(2)}) copy-start(f32[1,256]{1,0:T(1,128)} %constant.8.clone.scale_ref) | copy-start | bytes 3076
  5.6 45.8 %copy-start.6 = (s32[3]{0:T(128)S(1)}, s32[3]{0:T(128)}, u32[]{:S(2)}) copy-start(s32[3]{0:T(128)} %offsets_ref.1) | copy-start | bytes 40
  8.6 0.8 %copy-start.2 = (bf16[128,16,128]{2,1,0:T(8,128)(2,1)}, bf16[128,16,128]{2,1,0:T(8,128)(2,1)S(1)}, u32[]{:S(2)}) copy-start(bf16[128,16,128]{2,1,0:T(8,128)(2,1)S(1)} %whiten.1.send_ref) | copy-start | bytes 1572868
  51.4 1.7 %copy-start = (bf16[5,32,64,128]{3,2,1,0:T(8,128)(2,1)S(1)}, bf16[5,32,64,128]{3,2,1,0:T(8,128)(2,1)}, u32[]{:S(2)}) copy-start(bf16[5,32,64,128]{3,2,1,0:T(8,128)(2,1)} %exchange.1.own_ref.refs_0_.refs_1_.refs_2_) | copy-start | bytes 7864324

commit v2 on v1

--- a/solution.py
+++ b/solution.py
@@ -19,9 +19,14 @@
 EPSILON = 1e-06
 
 ROW_STEPS = 4
-CHUNKS = 4
+CHUNKS = 8
+AHEAD = 2
+LAG = 2
+DEPTH = 2
 BIN_BLOCK = 4
-VMEM_LIMIT = 40 * 1024 * 1024
+VMEM_LIMIT = 60 * 1024 * 1024
+CROSS_LIMIT = 40 * 1024 * 1024
+SMALL_LIMIT = 4 * 1024 * 1024
 MESH = pl.DeviceIdType.MESH
 
 
@@ -36,26 +41,33 @@
     return table.astype(np.float32).astype(ml_dtypes.bfloat16)
 
 
-def band_table():
-    idx = np.arange(BINS)
-    inside = (np.abs(idx[:, None] - idx[None, :]) <= SMOOTH).astype(np.float32)
-    band = np.concatenate([inside, np.ones((BINS, BINS), np.float32)], axis=1)
-    scale = np.concatenate(
-        [1.0 / inside.sum(axis=0), np.full((BINS,), WATER_LEVEL / BINS, np.float32)]
-    )
-    return band.astype(ml_dtypes.bfloat16), scale.astype(np.float32)[None, :]
-
-
-def whiten_kernel(wins, samples_ref, table_ref, band_ref, scale_ref, out_ref, white, turned):
+def band_weights():
+    source = lax.broadcasted_iota(jnp.int32, (BINS, 2 * BINS), 0)
+    target = lax.broadcasted_iota(jnp.int32, (BINS, 2 * BINS), 1)
+    inside = jnp.logical_or(jnp.abs(source - target) <= SMOOTH, target >= BINS)
+    return jnp.where(inside, 1.0, 0.0).astype(jnp.bfloat16)
+
+
+def band_scale():
+    bin_index = lax.broadcasted_iota(jnp.int32, (1, 2 * BINS), 1)
+    inside = jnp.minimum(bin_index, SMOOTH) + jnp.minimum(BINS - 1 - bin_index, SMOOTH) + 1
+    share = 1.0 / jnp.maximum(inside, 1).astype(jnp.float32)
+    return jnp.where(bin_index < BINS, share, WATER_LEVEL / BINS)
+
+
+def whiten_kernel(wins, samples_ref, table_ref, out_ref, white, turned):
     step = pl.program_id(0)
     rows = samples_ref.shape[0]
     channels = white.shape[1] // wins
     spectrum = jnp.dot(samples_ref[...], table_ref[...], preferred_element_type=jnp.float32)
     real, imag = spectrum[:, :BINS], spectrum[:, BINS:]
     energy = real * real + imag * imag
-    sums = jnp.dot(
-        energy.astype(jnp.bfloat16), band_ref[...], preferred_element_type=jnp.float32
-    ) * scale_ref[...]
+    high = energy.astype(jnp.bfloat16)
+    low = (energy - high.astype(jnp.float32)).astype(jnp.bfloat16)
+    weights = band_weights()
+    sums = jnp.dot(high, weights, preferred_element_type=jnp.float32)
+    sums += jnp.dot(low, weights, preferred_element_type=jnp.float32)
+    sums *= band_scale()
     factor = lax.rsqrt(sums[:, :BINS] + sums[:, BINS:] + EPSILON)
     here = pl.ds(pl.multiple_of(step * rows, rows), rows)
     white[0, here, :] = real * factor
@@ -74,7 +86,6 @@
     channels, wins, length = samples.shape
     rows = channels * wins
     table = jnp.asarray(dft_table(length))
-    band, scale = band_table()
     step_rows = rows // ROW_STEPS
     return pl.pallas_call(
         functools.partial(whiten_kernel, wins),
@@ -82,8 +93,6 @@
         in_specs=[
             pl.BlockSpec((step_rows, length), lambda i: (i, 0)),
             pl.BlockSpec((length, 2 * BINS), lambda i: (0, 0)),
-            pl.BlockSpec((BINS, 2 * BINS), lambda i: (0, 0)),
-            pl.BlockSpec((1, 2 * BINS), lambda i: (0, 0)),
         ],
         out_specs=pl.BlockSpec((BINS, 2 * wins, channels), lambda i: (0, 0, 0)),
         out_shape=jax.ShapeDtypeStruct((BINS, 2 * wins, channels), jnp.bfloat16),
@@ -93,7 +102,7 @@
         ],
         compiler_params=pltpu.CompilerParams(vmem_limit_bytes=VMEM_LIMIT),
         name="whiten",
-    )(samples.reshape(rows, length), table, jnp.asarray(band), jnp.asarray(scale))
+    )(samples.reshape(rows, length), table)
 
 
 def exchange_kernel(
@@ -162,89 +171,59 @@
     def across(at, c):
         return move(2 * at + 2 * (1 - odd), 2 * at + 1, partner, x_send, x_recv, at, c)
 
-    for c in range(CHUNKS):
-        for k in range(nw - 1):
-            spread(k, c).start()
+    both = jnp.logical_and(has_below, has_one)
+    odd_one = jnp.logical_and(is_odd, has_one)
+    even_one = jnp.logical_and(is_even, has_one)
+    even_two = jnp.logical_and(is_even, has_two)
+    items = 2 * CHUNKS
+
+    def sends(t):
+        found = []
+        if 0 <= t < items:
+            at, c = divmod(t, CHUNKS)
+            found.append(((has_below, both)[at], down(at, c)))
+            found.append(((is_odd, odd_one)[at], across(at, c)))
+        if 0 <= t - LAG < items:
+            at, c = divmod(t - LAG, CHUNKS)
+            found.append(((even_one, even_two)[at], across(at, c)))
+        return found
+
+    def guarded(when, action):
+        @pl.when(when)
+        def _():
+            action()
+
+    def start_spread(c):
+        if c < CHUNKS:
+            for k in range(nw - 1):
+                spread(k, c).start()
+
+    for c in range(AHEAD):
+        start_spread(c)
     home.wait()
-
-    def own_part(c):
-        for k in range(nw - 1):
-            spread(k, c).wait_recv()
-
-        @pl.when(has_below)
-        def _():
-            down(0, c).start()
-
-        @pl.when(is_odd)
-        def _():
-            across(0, c).start()
-
-    def second_part(c):
-        @pl.when(has_one)
-        def _():
-            down(0, c).wait_recv()
-
-            @pl.when(has_below)
-            def _():
-                down(1, c).start()
-
-            @pl.when(is_even)
-            def _():
-                across(0, c).start()
-
-            @pl.when(is_odd)
-            def _():
-                across(1, c).start()
-
-    def fourth_part(c):
-        @pl.when(has_two)
-        def _():
-            down(1, c).wait_recv()
-
-            @pl.when(is_even)
-            def _():
-                across(1, c).start()
-
-    own_part(0)
-    for c in range(1, CHUNKS):
-        own_part(c)
-        second_part(c - 1)
-    second_part(CHUNKS - 1)
-    for c in range(CHUNKS):
-        fourth_part(c)
-
+    steps = items + LAG
+    for t in range(steps):
+        if t < CHUNKS:
+            start_spread(t + AHEAD)
+            for k in range(nw - 1):
+                spread(k, t).wait_recv()
+        if 0 <= t - LAG < items:
+            at, c = divmod(t - LAG, CHUNKS)
+            guarded((has_one, has_two)[at], down(at, c).wait_recv)
+        for when, copy in sends(t - DEPTH):
+            guarded(when, copy.wait_send)
+        for when, copy in sends(t):
+            guarded(when, copy.start)
+    for t in range(steps - DEPTH, steps):
+        for when, copy in sends(t):
+            guarded(when, copy.wait_send)
     first_live = jnp.logical_or(is_even, has_one)
-    third_live = jnp.logical_or(jnp.logical_and(is_even, has_one), has_two)
-    first_sent = jnp.logical_or(is_odd, has_one)
-    third_sent = jnp.logical_or(jnp.logical_and(is_odd, has_one), has_two)
-    both = jnp.logical_and(has_below, has_one)
+    third_live = jnp.logical_or(even_one, has_two)
     for c in range(CHUNKS):
         for k in range(nw - 1):
             spread(k, c).wait_send()
-
-        @pl.when(first_live)
-        def _():
-            across(0, c).wait_recv()
-
-        @pl.when(third_live)
-        def _():
-            across(1, c).wait_recv()
-
-        @pl.when(has_below)
-        def _():
-            down(0, c).wait_send()
-
-        @pl.when(both)
-        def _():
-            down(1, c).wait_send()
-
-        @pl.when(first_sent)
-        def _():
-            across(0, c).wait_send()
-
-        @pl.when(third_sent)
-        def _():
-            across(1, c).wait_send()
+        guarded(first_live, across(0, c).wait_recv)
+        guarded(third_live, across(1, c).wait_recv)
 
 
 def exchange(white, nb, nw):
@@ -265,7 +244,9 @@
             pltpu.SemaphoreType.DMA((2, CHUNKS)),
             pltpu.SemaphoreType.DMA((2, CHUNKS)),
         ],
-        compiler_params=pltpu.CompilerParams(collective_id=0, has_side_effects=True),
+        compiler_params=pltpu.CompilerParams(
+            collective_id=0, has_side_effects=True, vmem_limit_bytes=SMALL_LIMIT
+        ),
         name="exchange",
     )(white)
 
@@ -278,13 +259,16 @@
     ]
     depth, channels = own_ref.shape[2], own_ref.shape[3]
     for b in range(own_ref.shape[1]):
-        mine = own_ref[0, b].astype(jnp.float32)
-        split = mine.reshape(depth // (2 * half), 2, half, channels)
-        swapped = jnp.stack([split[:, 1], -split[:, 0]], axis=1).reshape(depth, channels)
-        left = jnp.concatenate([mine.T, swapped.T], axis=0).astype(jnp.bfloat16)
+        left = own_ref[0, b].astype(jnp.float32).T.astype(jnp.bfloat16)
         for s, partner in enumerate(partners):
-            value = jnp.dot(left, partner[0, b], preferred_element_type=jnp.float32) * scales[s]
-            out_ref[s, b] = value.reshape(2, channels, channels).astype(jnp.bfloat16)
+            right = partner[0, b].astype(jnp.float32) * scales[s]
+            split = right.reshape(depth // (2 * half), 2, half, channels)
+            turned = jnp.stack([-split[:, 1], split[:, 0]], axis=1).reshape(depth, channels)
+            right = jnp.concatenate([right, turned], axis=1).astype(jnp.bfloat16)
+            value = jnp.dot(left, right, preferred_element_type=jnp.float32)
+            value = value.astype(jnp.bfloat16)
+            out_ref[s, b, 0] = value[:, :channels]
+            out_ref[s, b, 1] = value[:, channels:]
 
 
 def cross(near, pair_offsets, pair_count, wins):
@@ -311,7 +295,7 @@
             ),
         ),
         out_shape=jax.ShapeDtypeStruct((slots, bins_dev, 2, channels, channels), jnp.bfloat16),
-        compiler_params=pltpu.CompilerParams(vmem_limit_bytes=VMEM_LIMIT),
+        compiler_params=pltpu.CompilerParams(vmem_limit_bytes=CROSS_LIMIT),
         name="cross",
     )(pair_offsets, pair_count, *([near] * (slots + 1)))
 

time: 59.8 us -> 51.8 us (0.87)
  local copies, waits for them, and re-layouts: 7.45 us -> 1.05 us
  Pallas kernels: 51.3 us -> 49.8 us
    unnamed x14 -> x4, local copies, waits for them, and re-layouts: 7.45 us -> 1.05 us
    pallas_call x1, Pallas kernels: 42.1 us -> 37.4 us  [exchange(): pl.pallas_call(functools.partial(exchange_kernel, nb, nw), in_specs=[pl.B...]
    pallas_call x1, Pallas kernels: 2.95 us -> 6.3 us  [whiten(): pl.pallas_call(functools.partial(whiten_kernel, wins), grid=(ROW_STEPS,),...]
where the time goes in v2:
time: 51.8 us; the launch traced here: 51.6 us
  Pallas kernels  49.8 us (96%)
  local copies, waits for them, and re-layouts  1.05 us (2%)
  between operations  0.68 us (1%)
    pallas_call x1, Pallas kernels, exchange(): pl.pallas_call(functools.partial(exchange_kernel, nb, nw), in_specs=[pl.B...  37.4 us
    pallas_call x1, Pallas kernels, whiten(): pl.pallas_call(functools.partial(whiten_kernel, wins), grid=(ROW_STEPS,),...  6.3 us
    pallas_call x1, Pallas kernels, cross(): pl.pallas_call(functools.partial(cross_kernel, wins, depth // 2), grid_sp...  6.15 us
    unnamed x4, local copies, waits for them, and re-layouts  1.05 us

profile of v2, /device:TPU:0, one launch (start us, length us, event | category | flops | bytes accessed | tf_op | source)
XLA Modules:
  0.0 51.6 jit_solution(15836693140742388515)
XLA Ops:
  0.7 0.0 copy-start.1
  0.7 6.3 %whiten.1.send_ref = bf16[128,16,128]{2,1,0:T(8,128)(2,1)} custom-call(bf16[1024,2048]{1,0:T(8,128)(2,1)} %bitcast.1, bf16[2048,256]{1,0:T(8,128)(2,1)} %constant.2.clone.table_ref), custom_call_target="tpu_custom_call" | custom-call | tf_op jit(solution)/shard_map/whiten/pallas_call | solution.py:90
  7.0 0.0 copy-start
  7.0 1.0 %copy-done = bf16[128,16,128]{2,1,0:T(8,128)(2,1)S(1)} copy-done((bf16[128,16,128]{2,1,0:T(8,128)(2,1)S(1)}, bf16[128,16,128]{2,1,0:T(8,128)(2,1)}, u32[]{:S(2)}) %copy-start) | copy-done | bytes 524312
  8.0 37.4 %exchange.1.own_ref.refs_0_.refs_1_.refs_2_ = bf16[5,32,64,128]{3,2,1,0:T(8,128)(2,1)S(1)} custom-call(bf16[128,16,128]{2,1,0:T(8,128)(2,1)S(1)} %copy-done), custom_call_target="tpu_custom_call" | custom-call | tf_op jit(solution)/shard_map/exchange/pallas_call | solution.py:231
  45.4 0.0 copy-done.1
  45.4 6.2 %cross.1 = bf16[3,32,2,128,128]{4,3,2,1,0:T(8,128)(2,1)} custom-call(s32[3]{0:T(128)S(1)} %copy-done.1, s32[1]{0:T(128)S(6)} %copy.5.count_ref, bf16[5,32,64,128]{3,2,1,0:T(8,128)(2,1)S(1)} %exchange.1.own_ref.refs_0_.refs_1_.refs_2_, bf16[5,32,64,128]{3,2,1,0:T(8,128)(2,1)S(1)} %exchange.1.own_ref.refs_0_.refs_1_.refs_2_, ...), custom_call_target="tpu_custom_call" | custom-call | tf_op jit(solution)/shard_map/cross/pallas_call | solution.py:283
Async XLA Ops:
  0.7 44.8 %copy-start.1 = (s32[3]{0:T(128)S(1)}, s32[3]{0:T(128)}, u32[]{:S(2)}) copy-start(s32[3]{0:T(128)} %offsets_ref.1) | copy-start | bytes 40
  7.0 1.0 %copy-start = (bf16[128,16,128]{2,1,0:T(8,128)(2,1)S(1)}, bf16[128,16,128]{2,1,0:T(8,128)(2,1)}, u32[]{:S(2)}) copy-start(bf16[128,16,128]{2,1,0:T(8,128)(2,1)} %whiten.1.send_ref) | copy-start | bytes 1572868

commit v3 on v2

--- a/solution.py
+++ b/solution.py
@@ -18,12 +18,12 @@
 WATER_LEVEL = 0.1
 EPSILON = 1e-06
 
-ROW_STEPS = 4
+ROW_STEPS = 2
 CHUNKS = 8
 AHEAD = 2
 LAG = 2
 DEPTH = 2
-BIN_BLOCK = 4
+BIN_BLOCK = 16
 VMEM_LIMIT = 60 * 1024 * 1024
 CROSS_LIMIT = 40 * 1024 * 1024
 SMALL_LIMIT = 4 * 1024 * 1024

time: 51.8 us -> 49 us (0.946)
  Pallas kernels: 49.8 us -> 47.1 us
    pallas_call x1, Pallas kernels: 6.15 us -> 4.31 us  [cross(): pl.pallas_call(functools.partial(cross_kernel, wins, depth // 2), grid_sp...]
    pallas_call x1, Pallas kernels: 6.3 us -> 5.4 us  [whiten(): pl.pallas_call(functools.partial(whiten_kernel, wins), grid=(ROW_STEPS,),...]
where the time goes in v3:
time: 49 us; the launch traced here: 48.8 us
  Pallas kernels  47.1 us (96%)
  local copies, waits for them, and re-layouts  1.05 us (2%)
  between operations  0.68 us (1%)
    pallas_call x1, Pallas kernels, exchange(): pl.pallas_call(functools.partial(exchange_kernel, nb, nw), in_specs=[pl.B...  37.4 us
    pallas_call x1, Pallas kernels, whiten(): pl.pallas_call(functools.partial(whiten_kernel, wins), grid=(ROW_STEPS,),...  5.4 us
    pallas_call x1, Pallas kernels, cross(): pl.pallas_call(functools.partial(cross_kernel, wins, depth // 2), grid_sp...  4.31 us
    unnamed x4, local copies, waits for them, and re-layouts  1.05 us

profile of v3, /device:TPU:0, one launch (start us, length us, event | category | flops | bytes accessed | tf_op | source)
XLA Modules:
  0.0 48.8 jit_solution(17496027403167750115)
XLA Ops:
  0.7 0.0 copy-start.1
  0.7 5.4 %whiten.1.send_ref = bf16[128,16,128]{2,1,0:T(8,128)(2,1)} custom-call(bf16[1024,2048]{1,0:T(8,128)(2,1)} %bitcast.1, bf16[2048,256]{1,0:T(8,128)(2,1)} %constant.2.clone.table_ref), custom_call_target="tpu_custom_call" | custom-call | tf_op jit(solution)/shard_map/whiten/pallas_call | solution.py:90
  6.1 0.0 copy-start
  6.1 1.0 %copy-done = bf16[128,16,128]{2,1,0:T(8,128)(2,1)S(1)} copy-done((bf16[128,16,128]{2,1,0:T(8,128)(2,1)S(1)}, bf16[128,16,128]{2,1,0:T(8,128)(2,1)}, u32[]{:S(2)}) %copy-start) | copy-done | bytes 524312
  7.1 37.4 %exchange.1.own_ref.refs_0_.refs_1_.refs_2_ = bf16[5,32,64,128]{3,2,1,0:T(8,128)(2,1)S(1)} custom-call(bf16[128,16,128]{2,1,0:T(8,128)(2,1)S(1)} %copy-done), custom_call_target="tpu_custom_call" | custom-call | tf_op jit(solution)/shard_map/exchange/pallas_call | solution.py:231
  44.5 0.0 copy-done.1
  44.5 4.3 %cross.1 = bf16[3,32,2,128,128]{4,3,2,1,0:T(8,128)(2,1)} custom-call(s32[3]{0:T(128)S(1)} %copy-done.1, s32[1]{0:T(128)S(6)} %copy.5.count_ref, bf16[5,32,64,128]{3,2,1,0:T(8,128)(2,1)S(1)} %exchange.1.own_ref.refs_0_.refs_1_.refs_2_, bf16[5,32,64,128]{3,2,1,0:T(8,128)(2,1)S(1)} %exchange.1.own_ref.refs_0_.refs_1_.refs_2_, ...), custom_call_target="tpu_custom_call" | custom-call | tf_op jit(solution)/shard_map/cross/pallas_call | solution.py:283
Async XLA Ops:
  0.7 43.9 %copy-start.1 = (s32[3]{0:T(128)S(1)}, s32[3]{0:T(128)}, u32[]{:S(2)}) copy-start(s32[3]{0:T(128)} %offsets_ref.1) | copy-start | bytes 40
  6.1 1.0 %copy-start = (bf16[128,16,128]{2,1,0:T(8,128)(2,1)S(1)}, bf16[128,16,128]{2,1,0:T(8,128)(2,1)}, u32[]{:S(2)}) copy-start(bf16[128,16,128]{2,1,0:T(8,128)(2,1)} %whiten.1.send_ref) | copy-start | bytes 1572868

commit v4 on v3

--- a/solution.py
+++ b/solution.py
@@ -21,12 +21,11 @@
 ROW_STEPS = 2
 CHUNKS = 8
 AHEAD = 2
-LAG = 2
+LAG = 3
 DEPTH = 2
 BIN_BLOCK = 16
-VMEM_LIMIT = 60 * 1024 * 1024
 CROSS_LIMIT = 40 * 1024 * 1024
-SMALL_LIMIT = 4 * 1024 * 1024
+SMALL_LIMIT = 24 * 1024 * 1024
 MESH = pl.DeviceIdType.MESH
 
 
@@ -55,59 +54,45 @@
     return jnp.where(bin_index < BINS, share, WATER_LEVEL / BINS)
 
 
-def whiten_kernel(wins, samples_ref, table_ref, out_ref, white, turned):
-    step = pl.program_id(0)
-    rows = samples_ref.shape[0]
+def whiten(wins, copies, samples, table, white, turned, out):
     channels = white.shape[1] // wins
-    spectrum = jnp.dot(samples_ref[...], table_ref[...], preferred_element_type=jnp.float32)
-    real, imag = spectrum[:, :BINS], spectrum[:, BINS:]
-    energy = real * real + imag * imag
-    high = energy.astype(jnp.bfloat16)
-    low = (energy - high.astype(jnp.float32)).astype(jnp.bfloat16)
-    weights = band_weights()
-    sums = jnp.dot(high, weights, preferred_element_type=jnp.float32)
-    sums += jnp.dot(low, weights, preferred_element_type=jnp.float32)
-    sums *= band_scale()
-    factor = lax.rsqrt(sums[:, :BINS] + sums[:, BINS:] + EPSILON)
-    here = pl.ds(pl.multiple_of(step * rows, rows), rows)
-    white[0, here, :] = real * factor
-    white[1, here, :] = imag * factor
-
-    @pl.when(step == pl.num_programs(0) - 1)
-    def _():
-        for part in range(2):
-            for win in range(wins):
-                piece = white[part, pl.ds(win, channels, stride=wins), :]
-                turned[pl.ds(part * wins + win, BINS, stride=2 * wins), :] = piece.T
-        out_ref[...] = turned[...].reshape(out_ref.shape).astype(jnp.bfloat16)
-
-
-def whiten(samples):
-    channels, wins, length = samples.shape
-    rows = channels * wins
-    table = jnp.asarray(dft_table(length))
-    step_rows = rows // ROW_STEPS
-    return pl.pallas_call(
-        functools.partial(whiten_kernel, wins),
-        grid=(ROW_STEPS,),
-        in_specs=[
-            pl.BlockSpec((step_rows, length), lambda i: (i, 0)),
-            pl.BlockSpec((length, 2 * BINS), lambda i: (0, 0)),
-        ],
-        out_specs=pl.BlockSpec((BINS, 2 * wins, channels), lambda i: (0, 0, 0)),
-        out_shape=jax.ShapeDtypeStruct((BINS, 2 * wins, channels), jnp.bfloat16),
-        scratch_shapes=[
-            pltpu.VMEM((2, rows, BINS), jnp.float32),
-            pltpu.VMEM((BINS * 2 * wins, channels), jnp.float32),
-        ],
-        compiler_params=pltpu.CompilerParams(vmem_limit_bytes=VMEM_LIMIT),
-        name="whiten",
-    )(samples.reshape(rows, length), table)
+    rows = samples.shape[0] // ROW_STEPS
+    weights, scale = band_weights(), band_scale()
+    for step in range(ROW_STEPS):
+        copies[step].wait()
+        here = pl.ds(step * rows, rows)
+        spectrum = jnp.dot(samples[here, :], table[...], preferred_element_type=jnp.float32)
+        real, imag = spectrum[:, :BINS], spectrum[:, BINS:]
+        energy = real * real + imag * imag
+        high = energy.astype(jnp.bfloat16)
+        low = (energy - high.astype(jnp.float32)).astype(jnp.bfloat16)
+        sums = jnp.dot(high, weights, preferred_element_type=jnp.float32)
+        sums += jnp.dot(low, weights, preferred_element_type=jnp.float32)
+        sums *= scale
+        factor = lax.rsqrt(sums[:, :BINS] + sums[:, BINS:] + EPSILON)
+        white[0, here, :] = real * factor
+        white[1, here, :] = imag * factor
+    for part in range(2):
+        for win in range(wins):
+            piece = white[part, pl.ds(win, channels, stride=wins), :]
+            turned[pl.ds(part * wins + win, BINS, stride=2 * wins), :] = piece.T
+    out[...] = turned[...].reshape(out.shape).astype(jnp.bfloat16)
 
 
 def exchange_kernel(
-    nb, nw, send_ref, near_ref, home_sem, a_send, a_recv, z_send, z_recv, x_send, x_recv
+    nb, nw, wins, samples_ref, table_ref, near_ref, samples, table, white, turned, send_ref,
+    load_sem, table_sem, home_sem, a_send, a_recv, z_send, z_recv, x_send, x_recv
 ):
+    load_rows = samples.shape[0] // ROW_STEPS
+    table_load = pltpu.make_async_copy(table_ref, table, table_sem)
+    table_load.start()
+    loads = []
+    for step in range(ROW_STEPS):
+        here = pl.ds(step * load_rows, load_rows)
+        loads.append(
+            pltpu.make_async_copy(samples_ref.at[here], samples.at[here], load_sem.at[step])
+        )
+        loads[step].start()
     worker, group = lax.axis_index("blk"), lax.axis_index("win")
     level, odd = lax.div(worker, 2), lax.rem(worker, 2)
     levels = nb // 2
@@ -137,6 +122,9 @@
     @pl.when(has_one)
     def _():
         greet({"blk": worker + 2})
+
+    table_load.wait()
+    whiten(wins, loads, samples, table, white, turned, send_ref)
 
     my_rows = pl.ds(pl.multiple_of(group * rows, rows), rows)
     home = pltpu.make_async_copy(
@@ -226,16 +214,24 @@
         guarded(third_live, across(1, c).wait_recv)
 
 
-def exchange(white, nb, nw):
-    bins, rows, channels = white.shape
+def exchange(samples, nb, nw):
+    channels, wins, length = samples.shape
+    all_rows, rows = channels * wins, 2 * wins
     return pl.pallas_call(
-        functools.partial(exchange_kernel, nb, nw),
-        in_specs=[pl.BlockSpec(memory_space=pl.ANY)],
-        out_specs=pl.BlockSpec(memory_space=pl.ANY),
+        functools.partial(exchange_kernel, nb, nw, wins),
+        in_specs=[pl.BlockSpec(memory_space=pltpu.HBM)] * 2,
+        out_specs=pl.BlockSpec(memory_space=pltpu.VMEM),
         out_shape=jax.ShapeDtypeStruct(
-            (OFFSET + 1, bins // nw, nw * rows, channels), jnp.bfloat16
+            (OFFSET + 1, BINS // nw, nw * rows, channels), jnp.bfloat16
         ),
         scratch_shapes=[
+            pltpu.VMEM((all_rows, length), jnp.bfloat16),
+            pltpu.VMEM((length, 2 * BINS), jnp.bfloat16),
+            pltpu.VMEM((2, all_rows, BINS), jnp.float32),
+            pltpu.VMEM((BINS * rows, channels), jnp.float32),
+            pltpu.VMEM((BINS, rows, channels), jnp.bfloat16),
+            pltpu.SemaphoreType.DMA((ROW_STEPS,)),
+            pltpu.SemaphoreType.DMA,
             pltpu.SemaphoreType.DMA,
             pltpu.SemaphoreType.DMA((nw - 1, CHUNKS)),
             pltpu.SemaphoreType.DMA((nw - 1, CHUNKS)),
@@ -248,7 +244,7 @@
             collective_id=0, has_side_effects=True, vmem_limit_bytes=SMALL_LIMIT
         ),
         name="exchange",
-    )(white)
+    )(samples.reshape(all_rows, length), jnp.asarray(dft_table(length)))
 
 
 def cross_kernel(half, windows, offsets_ref, count_ref, own_ref, *refs):
@@ -301,8 +297,7 @@
 
 
 def shards(nb, nw, samples, pair_offsets, pair_count):
-    white = whiten(samples)
-    near = exchange(white, nb, nw)
+    near = exchange(samples, nb, nw)
     return cross(near, pair_offsets, pair_count, samples.shape[1])
 
 

time: 49 us -> 46.1 us (0.941)
  Pallas kernels: 47.1 us -> 41.8 us
  local copies, waits for them, and re-layouts: 1.05 us -> 3.41 us
    pallas_call x2 -> x1, Pallas kernels: 42.8 us -> 37.5 us  [exchange(): pl.pallas_call(functools.partial(exchange_kernel, nb, nw, wins), in_specs...]
    unnamed x4 -> x6, local copies, waits for them, and re-layouts: 1.05 us -> 3.41 us
where the time goes in v4:
time: 46.1 us; the launch traced here: 45.9 us
  Pallas kernels  41.8 us (91%)
  local copies, waits for them, and re-layouts  3.41 us (7%)
  between operations  0.69 us (1%)
    pallas_call x1, Pallas kernels, exchange(): pl.pallas_call(functools.partial(exchange_kernel, nb, nw, wins), in_specs...  37.5 us
    pallas_call x1, Pallas kernels, cross(): pl.pallas_call(functools.partial(cross_kernel, wins, depth // 2), grid_sp...  4.32 us
    unnamed x6, local copies, waits for them, and re-layouts  3.41 us

profile of v4, /device:TPU:0, one launch (start us, length us, event | category | flops | bytes accessed | tf_op | source)
XLA Modules:
  0.0 45.9 jit_solution(11496269676234804143)
XLA Ops:
  0.0 0.0 copy-start.2
  0.7 0.0 copy-start
  0.7 2.2 %copy-done = bf16[128,8,2048]{2,1,0:T(8,128)(2,1)S(1)} copy-done((bf16[128,8,2048]{2,1,0:T(8,128)(2,1)S(1)}, bf16[128,8,2048]{2,1,0:T(8,128)(2,1)}, u32[]{:S(2)}) %copy-start) | copy-done | bytes 4194328
  2.9 0.0 copy-start.1
  2.9 1.2 %copy-done.1 = bf16[2048,256]{1,0:T(8,128)(2,1)S(1)} copy-done((bf16[2048,256]{1,0:T(8,128)(2,1)S(1)}, bf16[2048,256]{1,0:T(8,128)(2,1)}, u32[]{:S(2)}) %copy-start.1) | copy-done | bytes 1048600
  4.1 37.5 %exchange.1.own_ref.refs_0_.refs_1_.refs_2_ = bf16[5,32,64,128]{3,2,1,0:T(8,128)(2,1)S(1)} custom-call(bf16[1024,2048]{1,0:T(8,128)(2,1)S(1)} %bitcast.1, bf16[2048,256]{1,0:T(8,128)(2,1)S(1)} %copy-done.1), custom_call_target="tpu_custom_call" | custom-call | tf_op jit(solution)/shard_map/exchange/pallas_call | solution.py:220
  41.6 0.0 copy-done.2
  41.6 4.3 %cross.1 = bf16[3,32,2,128,128]{4,3,2,1,0:T(8,128)(2,1)} custom-call(s32[3]{0:T(128)S(1)} %copy-done.2, s32[1]{0:T(128)S(6)} %copy.5.count_ref, bf16[5,32,64,128]{3,2,1,0:T(8,128)(2,1)S(1)} %exchange.1.own_ref.refs_0_.refs_1_.refs_2_, bf16[5,32,64,128]{3,2,1,0:T(8,128)(2,1)S(1)} %exchange.1.own_ref.refs_0_.refs_1_.refs_2_, ...), custom_call_target="tpu_custom_call" | custom-call | tf_op jit(solution)/shard_map/cross/pallas_call | solution.py:279
Async XLA Ops:
  0.0 41.6 %copy-start.2 = (s32[3]{0:T(128)S(1)}, s32[3]{0:T(128)}, u32[]{:S(2)}) copy-start(s32[3]{0:T(128)} %offsets_ref.1) | copy-start | bytes 40
  0.7 2.2 %copy-start = (bf16[128,8,2048]{2,1,0:T(8,128)(2,1)S(1)}, bf16[128,8,2048]{2,1,0:T(8,128)(2,1)}, u32[]{:S(2)}) copy-start(bf16[128,8,2048]{2,1,0:T(8,128)(2,1)} %param.4) | copy-start | bytes 12582916
  2.9 1.2 %copy-start.1 = (bf16[2048,256]{1,0:T(8,128)(2,1)S(1)}, bf16[2048,256]{1,0:T(8,128)(2,1)}, u32[]{:S(2)}) copy-start(bf16[2048,256]{1,0:T(8,128)(2,1)} %constant.2.clone.table_ref) | copy-start | bytes 3145732

commit v5 on v4

--- a/solution.py
+++ b/solution.py
@@ -18,10 +18,10 @@
 WATER_LEVEL = 0.1
 EPSILON = 1e-06
 
-ROW_STEPS = 2
+ROW_STEPS = 1
 CHUNKS = 8
 AHEAD = 2
-LAG = 3
+LAG = 4
 DEPTH = 2
 BIN_BLOCK = 16
 CROSS_LIMIT = 40 * 1024 * 1024

time: 46.1 us -> 44.8 us (0.972)
  Pallas kernels: 41.8 us -> 40.2 us
    pallas_call x1, Pallas kernels: 37.5 us -> 35.9 us  [exchange(): pl.pallas_call(functools.partial(exchange_kernel, nb, nw, wins), in_specs...]
where the time goes in v5:
time: 44.8 us; the launch traced here: 44.3 us
  Pallas kernels  40.2 us (90%)
  local copies, waits for them, and re-layouts  3.41 us (8%)
  between operations  0.69 us (2%)
    pallas_call x1, Pallas kernels, exchange(): pl.pallas_call(functools.partial(exchange_kernel, nb, nw, wins), in_specs...  35.9 us
    pallas_call x1, Pallas kernels, cross(): pl.pallas_call(functools.partial(cross_kernel, wins, depth // 2), grid_sp...  4.31 us
    unnamed x6, local copies, waits for them, and re-layouts  3.41 us

profile of v5, /device:TPU:0, one launch (start us, length us, event | category | flops | bytes accessed | tf_op | source)
XLA Modules:
  0.0 44.3 jit_solution(7124525812823435703)
XLA Ops:
  0.0 0.0 copy-start.2
  0.7 0.0 copy-start
  0.7 2.2 %copy-done = bf16[128,8,2048]{2,1,0:T(8,128)(2,1)S(1)} copy-done((bf16[128,8,2048]{2,1,0:T(8,128)(2,1)S(1)}, bf16[128,8,2048]{2,1,0:T(8,128)(2,1)}, u32[]{:S(2)}) %copy-start) | copy-done | bytes 4194328
  2.9 0.0 copy-start.1
  2.9 1.2 %copy-done.1 = bf16[2048,256]{1,0:T(8,128)(2,1)S(1)} copy-done((bf16[2048,256]{1,0:T(8,128)(2,1)S(1)}, bf16[2048,256]{1,0:T(8,128)(2,1)}, u32[]{:S(2)}) %copy-start.1) | copy-done | bytes 1048600
  4.1 35.9 %exchange.1.own_ref.refs_0_.refs_1_.refs_2_ = bf16[5,32,64,128]{3,2,1,0:T(8,128)(2,1)S(1)} custom-call(bf16[1024,2048]{1,0:T(8,128)(2,1)S(1)} %bitcast.1, bf16[2048,256]{1,0:T(8,128)(2,1)S(1)} %copy-done.1), custom_call_target="tpu_custom_call" | custom-call | tf_op jit(solution)/shard_map/exchange/pallas_call | solution.py:220
  40.0 0.0 copy-done.2
  40.0 4.3 %cross.1 = bf16[3,32,2,128,128]{4,3,2,1,0:T(8,128)(2,1)} custom-call(s32[3]{0:T(128)S(1)} %copy-done.2, s32[1]{0:T(128)S(6)} %copy.5.count_ref, bf16[5,32,64,128]{3,2,1,0:T(8,128)(2,1)S(1)} %exchange.1.own_ref.refs_0_.refs_1_.refs_2_, bf16[5,32,64,128]{3,2,1,0:T(8,128)(2,1)S(1)} %exchange.1.own_ref.refs_0_.refs_1_.refs_2_, ...), custom_call_target="tpu_custom_call" | custom-call | tf_op jit(solution)/shard_map/cross/pallas_call | solution.py:279
Async XLA Ops:
  0.0 40.0 %copy-start.2 = (s32[3]{0:T(128)S(1)}, s32[3]{0:T(128)}, u32[]{:S(2)}) copy-start(s32[3]{0:T(128)} %offsets_ref.1) | copy-start | bytes 40
  0.7 2.2 %copy-start = (bf16[128,8,2048]{2,1,0:T(8,128)(2,1)S(1)}, bf16[128,8,2048]{2,1,0:T(8,128)(2,1)}, u32[]{:S(2)}) copy-start(bf16[128,8,2048]{2,1,0:T(8,128)(2,1)} %param.4) | copy-start | bytes 12582916
  2.9 1.2 %copy-start.1 = (bf16[2048,256]{1,0:T(8,128)(2,1)S(1)}, bf16[2048,256]{1,0:T(8,128)(2,1)}, u32[]{:S(2)}) copy-start(bf16[2048,256]{1,0:T(8,128)(2,1)} %constant.2.clone.table_ref) | copy-start | bytes 3145732
